TPU v7x, 32 devices: a whole 2x2x4 slice. The times are simulated.
32 devices in a mesh: ctx: 16 (over z, y, x), tp: 2 (over core).
Axes of the slice: x: 2, y: 2, z: 4, core: 2. Of those that a mesh axis runs over, the one named last changes fastest.
Arguments:
- q_one: bfloat16 [4096, 8192], P('ctx', 'tp'), may hold values from -6 to 6
- k_one: bfloat16 [4096, 8192], P('ctx', 'tp'), may hold values from -40 to 40, as said below
- v_one: bfloat16 [4096, 8192], P('ctx', 'tp'), may hold values from -6 to 6
- mr_filter: bfloat16 [512, 128], P('tp'), may hold values from -3.535534 to 3.535534
- norm_gain: float32 [8192], P('tp'), may hold values from 0.1 to 1.9
- q_two: bfloat16 [4096, 8192], P('ctx', 'tp'), may hold values from -6 to 6
- k_two: bfloat16 [4096, 8192], P('ctx', 'tp'), may hold values from -6 to 6
- li_rates: float32 [16, 8192], P(None, 'tp'), may hold values from 6.1035156e-05 to 0.03
- li_residues: float32 [16, 8192], P(None, 'tp'), may hold values from -4 to 4
Outputs:
- mixed: bfloat16 [4096, 8192], P('ctx', 'tp')
Inputs may be any that keep to these rules, and one draw needn't show every extreme that they name: Each row of k_one has a scale of its own.
All inputs are finite; a program needn't handle non-finite values.
Results may differ from a plain program's by a relative error of at most 0.0057.
Values may be sent and summed in bfloat16 or wider, within the bound.
A program may use at most 128 MiB of HBM per device.

v0:
```python
import functools
import jax
import jax.numpy as jnp
from jax import lax
from jax.experimental import pallas as pl
from jax.experimental.pallas import tpu as pltpu
from jax.sharding import PartitionSpec as P

D = 8192
LANES = 128
SEGS = 8
F32 = jnp.float32
BF16 = jnp.bfloat16
MESH = pl.DeviceIdType.MESH
PIECES = 4


def toeplitz_rows(tap_rows, groups, earlier_store, own_store):
    taps = tap_rows.shape[1]
    row = lax.broadcasted_iota(jnp.int32, (taps, taps), 0)
    col = lax.broadcasted_iota(jnp.int32, (taps, taps), 1)
    later = col > row
    for g in range(groups):
        base = jnp.broadcast_to(tap_rows[g : g + 1, :], (8, taps))
        base = pltpu.roll(base, 0, 1, stride=1, stride_axis=0)
        tiles = [base if i == 0 else pltpu.roll(base, 8 * i, 1) for i in range(taps // 8)]
        circulant = jnp.concatenate(tiles, axis=0)
        rows = slice(g * taps, (g + 1) * taps)
        earlier_store[rows, :] = jnp.where(later, circulant, 0.0).astype(BF16)
        own_store[rows, :] = jnp.where(later, 0.0, circulant).astype(BF16)


def pick_groups(product, groups, taps):
    lane_group = lax.broadcasted_iota(jnp.int32, (taps, LANES), 1) // (LANES // groups)
    picked = product[:taps]
    for g in range(1, groups):
        picked = jnp.where(lane_group == g, product[g * taps : (g + 1) * taps], picked)
    return picked


def whole_kernel(
    ctx_size, tp_size, owners,
    q1_hbm, k1_hbm, v1_hbm, q2_hbm, k2_hbm, tap_ref, gain_ref, rate_ref, weight_ref,
    out_hbm,
    q1, k1, v1, q2, k2, out, u_one, halo, z, early, own_table, taps_f,
    squares, scale, u_wide, y_wide, prior, state, inbox, outbox, incoming,
    load_sem, halo_send, halo_recv, sq_send, sq_recv, in_send, in_recv, back_send, back_recv, out_sem,
):
    me = lax.axis_index("ctx")
    core = lax.axis_index("tp")
    length, channels = q1.shape
    filters, taps = tap_ref.shape
    modes = rate_ref.shape[0]
    chunks = channels // LANES
    groups = filters // chunks
    steps = length // SEGS
    own = channels // owners
    per_owner = own // LANES
    piece_width = channels // PIECES
    first, second = slice(0, taps), slice(taps, 2 * taps)

    barrier = pltpu.get_barrier_semaphore()

    @pl.loop(1, ctx_size)
    def _(k):
        pl.semaphore_signal(barrier, inc=1, device_id={"ctx": lax.rem(me + k, ctx_size)}, device_id_type=MESH)

    @pl.loop(1, tp_size)
    def _(k):
        pl.semaphore_signal(barrier, inc=1, device_id={"tp": lax.rem(core + k, tp_size)}, device_id_type=MESH)

    loads = [
        pltpu.make_async_copy(src.at[rows], dst.at[rows], load_sem.at[i])
        for i, (src, dst, rows) in enumerate([
            (k1_hbm, k1, pl.ds(taps, taps)), (v1_hbm, v1, pl.ds(taps, taps)),
            (k1_hbm, k1, pl.ds(0, taps)), (v1_hbm, v1, pl.ds(0, taps)),
            (q1_hbm, q1, pl.ds(0, length)), (k2_hbm, k2, pl.ds(0, length)),
            (q2_hbm, q2, pl.ds(0, length)),
        ])
    ]
    for load in loads:
        load.start()

    source = lax.broadcasted_iota(jnp.int32, (taps, taps), 0)
    target = lax.broadcasted_iota(jnp.int32, (taps, taps), 1)
    mirror = jnp.where(lax.rem(source + target, taps) == 0, 1.0, 0.0).astype(BF16)
    taps_f[...] = jnp.dot(tap_ref[...], mirror, preferred_element_type=F32)
    squares[core] = jnp.zeros((length, LANES), F32)

    def lanes_of(c):
        return pl.ds(pl.multiple_of(c * LANES, LANES), LANES)

    def gate(rows):
        @pl.loop(0, chunks)
        def _(c):
            at = lanes_of(c)
            u_one[rows, at] = (k1[rows, at].astype(F32) * v1[rows, at].astype(F32)).astype(BF16)

    loads[0].wait()
    loads[1].wait()
    gate(second)
    pl.semaphore_wait(barrier, ctx_size - 1 + tp_size - 1)

    def halo_copy(p):
        cols = pl.ds(p * piece_width, piece_width)
        return pltpu.make_async_remote_copy(
            src_ref=u_one.at[pl.ds(taps, taps), cols], dst_ref=halo.at[:, cols],
            send_sem=halo_send.at[p], recv_sem=halo_recv.at[p],
            device_id={"ctx": lax.rem(me + 1, ctx_size)}, device_id_type=MESH,
        )

    @pl.when(me < ctx_size - 1)
    def _():
        for p in range(PIECES):
            halo_copy(p).start()

    @pl.when(me == 0)
    def _():
        halo[...] = jnp.zeros_like(halo)

    loads[2].wait()
    loads[3].wait()
    gate(first)
    loads[4].wait()

    @pl.loop(0, chunks)
    def _(c):
        at = lanes_of(c)
        tap_rows = taps_f[pl.ds(pl.multiple_of(c * groups, groups), groups), :]
        toeplitz_rows(tap_rows, groups, early.at[c], own_table)
        left = jnp.concatenate([early[c], own_table[...]], axis=1)
        head, rest = u_one[first, at], u_one[second, at]
        right = jnp.concatenate([
            jnp.concatenate([jnp.zeros_like(head), head], axis=0),
            jnp.concatenate([head, rest], axis=0),
        ], axis=1)
        product = jnp.dot(left, right, preferred_element_type=F32)
        z[first, at] = pick_groups(product[:, :LANES], groups, taps)
        late = q1[second, at].astype(F32) * pick_groups(product[:, LANES:], groups, taps)
        z[second, at] = late
        squares[core, second, :] += late * late

    pairs = chunks // PIECES // 2
    for p in range(PIECES):
        @pl.when(me > 0)
        def _():
            halo_copy(p).wait_recv()

        @pl.loop(p * pairs, (p + 1) * pairs)
        def _(pair):
            left = jnp.concatenate([early[2 * pair], early[2 * pair + 1]], axis=1)
            one, two = halo[:, lanes_of(2 * pair)], halo[:, lanes_of(2 * pair + 1)]
            zero = jnp.zeros_like(one)
            right = jnp.concatenate([
                jnp.concatenate([one, zero], axis=0), jnp.concatenate([zero, two], axis=0)
            ], axis=1)
            product = jnp.dot(left, right, preferred_element_type=F32)
            for i in range(2):
                at = lanes_of(2 * pair + i)
                conv = z[first, at] + pick_groups(product[:, i * LANES : (i + 1) * LANES], groups, taps)
                value = q1[first, at].astype(F32) * conv
                z[first, at] = value
                squares[core, first, :] += value * value

    def square_copy(k, slot):
        return pltpu.make_async_remote_copy(
            src_ref=squares.at[core], dst_ref=squares.at[slot],
            send_sem=sq_send.at[k], recv_sem=sq_recv.at[slot],
            device_id={"tp": lax.rem(core + k, tp_size)}, device_id_type=MESH,
        )

    @pl.loop(1, tp_size)
    def _(k):
        square_copy(k, core).start()

    loads[5].wait()

    @pl.loop(1, tp_size)
    def _(k):
        square_copy(k, lax.rem(core + k, tp_size)).wait_recv()

    total = squares[0]
    for i in range(1, tp_size):
        total = total + squares[i]
    total = jnp.sum(total, axis=1, keepdims=True)
    scale[...] = jnp.broadcast_to(lax.rsqrt(total / D + 1e-06), (length, LANES))

    segment = lax.broadcasted_iota(jnp.int32, (SEGS, LANES), 0)

    def decays(at):
        return [jnp.broadcast_to(jnp.exp(-rate_ref[m : m + 1, at]), (SEGS, LANES)) for m in range(modes)]

    def in_copy(j):
        return pltpu.make_async_remote_copy(
            src_ref=state.at[j], dst_ref=inbox.at[me],
            send_sem=in_send.at[j], recv_sem=in_recv.at[me],
            device_id={"ctx": j}, device_id_type=MESH,
        )

    @pl.loop(0, owners)
    def _(k):
        j = lax.rem(me + 1 + k, owners)
        for i in range(per_owner):
            at = lanes_of(j * per_owner + i)
            scaled = z[:, at] * scale[...] * gain_ref[:, at]
            u_two = (k2[:, at].astype(F32) * scaled).astype(BF16).astype(F32)
            z[:, at] = u_two
            u_wide[i] = u_two
            decay = decays(at)

            def step(t, states):
                x = u_wide[i, pl.ds(t, SEGS, stride=steps), :]
                return tuple(decay[m] * states[m] + x for m in range(modes))

            states = lax.fori_loop(
                0, steps, step, (jnp.zeros((SEGS, LANES), F32),) * modes, unroll=8
            )
            for m in range(modes):
                inclusive = states[m]
                shift = 1
                while shift < SEGS:
                    factor = jnp.exp(-rate_ref[m : m + 1, at] * (steps * shift))
                    moved = jnp.where(segment >= shift, pltpu.roll(inclusive, shift, 0), 0.0)
                    inclusive = inclusive + factor * moved
                    shift *= 2
                prior[m * SEGS : (m + 1) * SEGS, at] = jnp.where(
                    segment >= 1, pltpu.roll(inclusive, 1, 0), 0.0
                )
                state[j, m : m + 1, i * LANES : (i + 1) * LANES] = inclusive[SEGS - 1 :, :]

        @pl.when(j != me)
        def _():
            in_copy(j).start()

    def in_arrival(d):
        return pltpu.make_async_remote_copy(
            src_ref=state.at[0], dst_ref=inbox.at[d],
            send_sem=in_send.at[0], recv_sem=in_recv.at[d],
            device_id={"ctx": d}, device_id_type=MESH,
        )

    def back_copy(d):
        return pltpu.make_async_remote_copy(
            src_ref=outbox.at[d], dst_ref=incoming.at[me],
            send_sem=back_send.at[d], recv_sem=back_recv.at[me],
            device_id={"ctx": d}, device_id_type=MESH,
        )

    def back_arrival(j):
        return pltpu.make_async_remote_copy(
            src_ref=outbox.at[0], dst_ref=incoming.at[j],
            send_sem=back_send.at[0], recv_sem=back_recv.at[j],
            device_id={"ctx": j}, device_id_type=MESH,
        )

    @pl.when(me < owners)
    def _():
        inbox[me] = state[lax.rem(me, owners)]
        mine = pl.ds(pl.multiple_of(lax.rem(me, owners) * own, own), own)
        stride = jnp.exp(-rate_ref[:, mine] * length)

        def pass_on(d, running):
            @pl.when(d != me)
            def _():
                in_arrival(d).wait_recv()
            outbox[d] = running

            @pl.when(d != me)
            def _():
                back_copy(d).start()

            @pl.when(d == me)
            def _():
                incoming[lax.rem(me, owners)] = running
            return stride * running + inbox[d]

        lax.fori_loop(0, ctx_size, pass_on, jnp.zeros((modes, own), F32))

    loads[6].wait()
    span = (segment * steps).astype(F32)

    def out_copy(j):
        cols = pl.ds(pl.multiple_of(j * own, own), own)
        return pltpu.make_async_copy(out.at[:, cols], out_hbm.at[:, cols], out_sem.at[j])

    @pl.loop(0, owners)
    def _(j):
        @pl.when(j != me)
        def _():
            back_arrival(j).wait_recv()
        for i in range(per_owner):
            at = lanes_of(j * per_owner + i)
            u_wide[i] = z[:, at]
            decay = decays(at)
            weight = [jnp.broadcast_to(weight_ref[m : m + 1, at], (SEGS, LANES)) for m in range(modes)]
            states = tuple(
                prior[m * SEGS : (m + 1) * SEGS, at]
                + jnp.exp(-rate_ref[m : m + 1, at] * span)
                * incoming[j, m : m + 1, i * LANES : (i + 1) * LANES]
                for m in range(modes)
            )

            def step(t, states):
                rows = pl.ds(t, SEGS, stride=steps)
                x = u_wide[i, rows, :]
                states = tuple(decay[m] * states[m] + x for m in range(modes))
                terms = [weight[m] * states[m] for m in range(modes)]
                while len(terms) > 1:
                    terms = [a + b for a, b in zip(terms[::2], terms[1::2])]
                y_wide[i, rows, :] = terms[0]
                return states

            lax.fori_loop(0, steps, step, states, unroll=8)
            out[:, at] = (q2[:, at].astype(F32) * y_wide[i]).astype(BF16)
        out_copy(j).start()

    @pl.loop(0, owners)
    def _(j):
        out_copy(j).wait()

        @pl.when(j != me)
        def _():
            in_copy(j).wait_send()

    @pl.when(me < owners)
    def _():
        @pl.loop(0, ctx_size)
        def _(d):
            @pl.when(d != me)
            def _():
                back_copy(d).wait_send()

    @pl.loop(1, tp_size)
    def _(k):
        square_copy(k, core).wait_send()

    @pl.when(me < ctx_size - 1)
    def _():
        for p in range(PIECES):
            halo_copy(p).wait_send()


def on_device(q_one, k_one, v_one, mr_filter, norm_gain, q_two, k_two, li_rates, li_residues):
    length, channels = q_one.shape
    filters, taps = mr_filter.shape
    modes = li_rates.shape[0]
    ctx_size, tp_size = lax.axis_size("ctx"), lax.axis_size("tp")
    owners = min(ctx_size, channels // LANES)
    own = channels // owners
    chunks = channels // LANES
    table_rows = filters // chunks * taps
    weights = li_residues * jnp.sqrt(-jnp.expm1(-2.0 * li_rates))
    wide = pltpu.VMEM((length, channels), BF16)
    dma = pltpu.SemaphoreType.DMA
    anywhere = pl.BlockSpec(memory_space=pl.ANY)
    inside = pl.BlockSpec(memory_space=pltpu.VMEM)
    return pl.pallas_call(
        functools.partial(whole_kernel, ctx_size, tp_size, owners),
        in_specs=[anywhere] * 5 + [inside] * 4,
        out_specs=anywhere,
        out_shape=jax.ShapeDtypeStruct((length, channels), BF16),
        scratch_shapes=[
            wide, wide, wide, wide, wide, wide, wide,
            pltpu.VMEM((taps, channels), BF16),
            pltpu.VMEM((length, channels), F32),
            pltpu.VMEM((chunks, table_rows, taps), BF16),
            pltpu.VMEM((table_rows, taps), BF16),
            pltpu.VMEM((filters, taps), F32),
            pltpu.VMEM((tp_size, length, LANES), F32),
            pltpu.VMEM((length, LANES), F32),
            pltpu.VMEM((own // LANES, length, LANES), F32),
            pltpu.VMEM((own // LANES, length, LANES), F32),
            pltpu.VMEM((modes * SEGS, channels), F32),
            pltpu.VMEM((owners, modes, own), F32),
            pltpu.VMEM((ctx_size, modes, own), F32),
            pltpu.VMEM((ctx_size, modes, own), F32),
            pltpu.VMEM((owners, modes, own), F32),
            dma((7,)), dma((PIECES,)), dma((PIECES,)), dma((tp_size,)), dma((tp_size,)),
            dma((owners,)), dma((ctx_size,)), dma((ctx_size,)), dma((owners,)), dma((owners,)),
        ],
        compiler_params=pltpu.CompilerParams(
            vmem_limit_bytes=60 << 20, collective_id=0, has_side_effects=True
        ),
    )(q_one, k_one, v_one, q_two, k_two, mr_filter, norm_gain[None, :], li_rates, weights)


def solution(mesh):
    in_specs = (
        P("ctx", "tp"),
        P("ctx", "tp"),
        P("ctx", "tp"),
        P("tp", None),
        P("tp"),
        P("ctx", "tp"),
        P("ctx", "tp"),
        P(None, "tp"),
        P(None, "tp"),
    )
    out_specs = P("ctx", "tp")
    return jax.shard_map(
        on_device, mesh=mesh, in_specs=in_specs, out_specs=out_specs, check_vma=False
    )
```

profile of v0, /device:TPU:31, one launch (start us, length us, event | category | flops | bytes accessed | tf_op | source)
XLA Modules:
  0.0 70.8 jit_solution(1091362020962395071)
XLA Ops:
  0.0 1.9 %sqrt_multiply_fusion.weight_ref = f32[16,4096]{1,0:T(8,128)} fusion(f32[16,4096]{1,0:T(8,128)} %param.17, f32[16,4096]{1,0:T(8,128)} %rate_ref.1), kind=kLoop, calls=%fused_computation | loop fusion | flops 196608 | bytes 786432 | tf_op jit(solution)/shard_map/mul | solution.py:352
  1.9 65.8 %shard_map.91 = bf16[256,4096]{1,0:T(8,128)(2,1)} custom-call(bf16[256,4096]{1,0:T(8,128)(2,1)} %q1_hbm.1, bf16[256,4096]{1,0:T(8,128)(2,1)} %k1_hbm.1, bf16[256,4096]{1,0:T(8,128)(2,1)} %v1_hbm.1, bf16[256,4096]{1,0:T(8,128)(2,1)} %q2_hbm.1, bf16[256,4096]{1,0:T(8,128)(2,1)} %k2_hbm.1, bf16[256,128]{1,0:T(8,128)(2,1)} %tap_ref.1, f32[1,4096]{1,0:T(1,128)} %bitcast.1, ...), custom_call_target="tpu_custom_call" | custom-call | tf_op jit(solution)/shard_map/pallas_call | solution.py:357
  67.7 3.1 %copy.11 = bf16[256,4096]{1,0:T(8,128)(2,1)} copy(bf16[256,4096]{1,0:T(8,128)(2,1)} %shard_map.91) | data formatting | bytes 4194304
where the time goes:
time: 71 us; the launch traced here: 70.8 us
  Pallas kernels  65.8 us (93%)
  local copies, waits for them, and re-layouts  3.13 us (4%)
  other arithmetic  1.89 us (3%)
    pallas_call x1, Pallas kernels, on_device(): pl.pallas_call(functools.partial(whole_kernel, ctx_size, tp_size, owners)...  65.8 us
    unnamed x1, local copies, waits for them, and re-layouts  3.13 us
    mul x1, other arithmetic, on_device(): weights = li_residues * jnp.sqrt(-jnp.expm1(-2.0 * li_rates))  1.89 us

commit v1 on v0

--- a/solution.py
+++ b/solution.py
@@ -40,10 +40,11 @@
 
 def whole_kernel(
     ctx_size, tp_size, owners,
-    q1_hbm, k1_hbm, v1_hbm, q2_hbm, k2_hbm, tap_ref, gain_ref, rate_ref, weight_ref,
+    q1_hbm, k1_hbm, v1_hbm, q2_hbm, k2_hbm, tap_ref, gain_ref, rate_ref, residue_ref,
     out_hbm,
     q1, k1, v1, q2, k2, out, u_one, halo, z, early, own_table, taps_f,
-    squares, scale, u_wide, y_wide, prior, state, inbox, outbox, incoming,
+    squares, scale, u_wide, y_wide, y, weights, prior, early_state, late_state, closing,
+    state, inbox, outbox, incoming,
     load_sem, halo_send, halo_recv, sq_send, sq_recv, in_send, in_recv, back_send, back_recv, out_sem,
 ):
     me = lax.axis_index("ctx")
@@ -53,7 +54,7 @@
     modes = rate_ref.shape[0]
     chunks = channels // LANES
     groups = filters // chunks
-    steps = length // SEGS
+    steps = taps // SEGS
     own = channels // owners
     per_owner = own // LANES
     piece_width = channels // PIECES
@@ -140,6 +141,109 @@
         z[second, at] = late
         squares[core, second, :] += late * late
 
+    segment = lax.broadcasted_iota(jnp.int32, (SEGS, LANES), 0)
+    span = (segment * steps).astype(F32)
+    halves = (first, second)
+
+    def square_copy(h, k, slot):
+        rows = pl.ds(h * taps, taps)
+        return pltpu.make_async_remote_copy(
+            src_ref=squares.at[core, rows], dst_ref=squares.at[slot, rows],
+            send_sem=sq_send.at[h, k], recv_sem=sq_recv.at[h, slot],
+            device_id={"tp": lax.rem(core + k, tp_size)}, device_id_type=MESH,
+        )
+
+    def send_squares(h):
+        @pl.loop(1, tp_size)
+        def _(k):
+            square_copy(h, k, core).start()
+
+    def find_scale(h):
+        @pl.loop(1, tp_size)
+        def _(k):
+            square_copy(h, k, lax.rem(core + k, tp_size)).wait_recv()
+        total = squares[0, halves[h], :]
+        for i in range(1, tp_size):
+            total = total + squares[i, halves[h], :]
+        total = jnp.sum(total, axis=1, keepdims=True)
+        scale[halves[h], :] = jnp.broadcast_to(lax.rsqrt(total / D + 1e-06), (taps, LANES))
+
+    def decays(at):
+        return [jnp.broadcast_to(jnp.exp(-rate_ref[m : m + 1, at]), (SEGS, LANES)) for m in range(modes)]
+
+    def set_signal(h, at, i):
+        scaled = z[halves[h], at] * scale[halves[h], :] * gain_ref[:, at]
+        u_two = (k2[halves[h], at].astype(F32) * scaled).astype(BF16).astype(F32)
+        z[halves[h], at] = u_two
+        u_wide[i] = u_two
+
+    zero_states = (jnp.zeros((SEGS, LANES), F32),) * modes
+
+    def local_pass(h, at, i):
+        decay = decays(at)
+        weight = [jnp.broadcast_to(weights[m : m + 1, at], (SEGS, LANES)) for m in range(modes)]
+
+        def step(t, states):
+            rows = pl.ds(t, SEGS, stride=steps)
+            x = u_wide[i, rows, :]
+            states = tuple(decay[m] * states[m] + x for m in range(modes))
+            terms = [weight[m] * states[m] for m in range(modes)]
+            while len(terms) > 1:
+                terms = [a + b for a, b in zip(terms[::2], terms[1::2])]
+            y_wide[i, rows, :] = terms[0]
+            return states
+
+        states = lax.fori_loop(0, steps, step, zero_states, unroll=8)
+        y[halves[h], at] = y_wide[i, :taps, :]
+        return states
+
+    def closing_pass(at, i):
+        decay = decays(at)
+
+        def step(t, states):
+            x = u_wide[i, pl.ds(t, SEGS, stride=steps), :]
+            return tuple(decay[m] * states[m] + x for m in range(modes))
+
+        return lax.fori_loop(0, steps, step, zero_states, unroll=16)
+
+    def join_segments(h, at, m, inclusive):
+        factor = jnp.exp(-rate_ref[m : m + 1, at] * steps)
+        shift = 1
+        while shift < SEGS:
+            moved = jnp.where(segment >= shift, pltpu.roll(inclusive, shift, 0), 0.0)
+            inclusive = inclusive + factor * moved
+            factor = factor * factor
+            shift *= 2
+        prior[h, m * SEGS : (m + 1) * SEGS, at] = jnp.where(
+            segment >= 1, pltpu.roll(inclusive, 1, 0), 0.0
+        )
+        return inclusive[SEGS - 1 :, :], factor
+
+    send_squares(1)
+
+    @pl.loop(0, chunks)
+    def _(c):
+        at = lanes_of(c)
+        double = 2.0 * rate_ref[:, at]
+        series = jnp.ones_like(double)
+        for order in range(10, 1, -1):
+            series = 1.0 - double * series * (1.0 / order)
+        gap = jnp.where(double < 0.5, double * series, 1.0 - jnp.exp(-double))
+        weights[:, at] = residue_ref[:, at] * jnp.sqrt(gap)
+
+    loads[5].wait()
+    find_scale(1)
+
+    @pl.loop(0, chunks // 2)
+    def _(pair):
+        for i in range(2):
+            at = lanes_of(2 * pair + i)
+            set_signal(1, at, i)
+            states = local_pass(1, at, i)
+            for m in range(modes):
+                last, _ = join_segments(1, at, m, states[m])
+                late_state[m : m + 1, at] = last
+
     pairs = chunks // PIECES // 2
     for p in range(PIECES):
         @pl.when(me > 0)
@@ -162,33 +266,8 @@
                 z[first, at] = value
                 squares[core, first, :] += value * value
 
-    def square_copy(k, slot):
-        return pltpu.make_async_remote_copy(
-            src_ref=squares.at[core], dst_ref=squares.at[slot],
-            send_sem=sq_send.at[k], recv_sem=sq_recv.at[slot],
-            device_id={"tp": lax.rem(core + k, tp_size)}, device_id_type=MESH,
-        )
-
-    @pl.loop(1, tp_size)
-    def _(k):
-        square_copy(k, core).start()
-
-    loads[5].wait()
-
-    @pl.loop(1, tp_size)
-    def _(k):
-        square_copy(k, lax.rem(core + k, tp_size)).wait_recv()
-
-    total = squares[0]
-    for i in range(1, tp_size):
-        total = total + squares[i]
-    total = jnp.sum(total, axis=1, keepdims=True)
-    scale[...] = jnp.broadcast_to(lax.rsqrt(total / D + 1e-06), (length, LANES))
-
-    segment = lax.broadcasted_iota(jnp.int32, (SEGS, LANES), 0)
-
-    def decays(at):
-        return [jnp.broadcast_to(jnp.exp(-rate_ref[m : m + 1, at]), (SEGS, LANES)) for m in range(modes)]
+    send_squares(0)
+    find_scale(0)
 
     def in_copy(j):
         return pltpu.make_async_remote_copy(
@@ -202,36 +281,26 @@
         j = lax.rem(me + 1 + k, owners)
         for i in range(per_owner):
             at = lanes_of(j * per_owner + i)
-            scaled = z[:, at] * scale[...] * gain_ref[:, at]
-            u_two = (k2[:, at].astype(F32) * scaled).astype(BF16).astype(F32)
-            z[:, at] = u_two
-            u_wide[i] = u_two
-            decay = decays(at)
-
-            def step(t, states):
-                x = u_wide[i, pl.ds(t, SEGS, stride=steps), :]
-                return tuple(decay[m] * states[m] + x for m in range(modes))
-
-            states = lax.fori_loop(
-                0, steps, step, (jnp.zeros((SEGS, LANES), F32),) * modes, unroll=8
-            )
+            set_signal(0, at, i)
+            states = closing_pass(at, i)
             for m in range(modes):
-                inclusive = states[m]
-                shift = 1
-                while shift < SEGS:
-                    factor = jnp.exp(-rate_ref[m : m + 1, at] * (steps * shift))
-                    moved = jnp.where(segment >= shift, pltpu.roll(inclusive, shift, 0), 0.0)
-                    inclusive = inclusive + factor * moved
-                    shift *= 2
-                prior[m * SEGS : (m + 1) * SEGS, at] = jnp.where(
-                    segment >= 1, pltpu.roll(inclusive, 1, 0), 0.0
-                )
-                state[j, m : m + 1, i * LANES : (i + 1) * LANES] = inclusive[SEGS - 1 :, :]
+                last, factor = join_segments(0, at, m, states[m])
+                early_state[m : m + 1, at] = last
+                closing[m : m + 1, :] = factor * last + late_state[m : m + 1, at]
+            state[j, :, i * LANES : (i + 1) * LANES] = closing[...].astype(BF16)
 
         @pl.when(j != me)
         def _():
             in_copy(j).start()
 
+    def local_first(start, stop):
+        @pl.loop(start, stop)
+        def _(pair):
+            for i in range(2):
+                at = lanes_of(2 * pair + i)
+                u_wide[i] = z[first, at]
+                local_pass(0, at, i)
+
     def in_arrival(d):
         return pltpu.make_async_remote_copy(
             src_ref=state.at[0], dst_ref=inbox.at[d],
@@ -252,6 +321,9 @@
             send_sem=back_send.at[0], recv_sem=back_recv.at[j],
             device_id={"ctx": j}, device_id_type=MESH,
         )
+
+    early_pairs = chunks // 4
+    local_first(0, early_pairs)
 
     @pl.when(me < owners)
     def _():
@@ -263,7 +335,8 @@
             @pl.when(d != me)
             def _():
                 in_arrival(d).wait_recv()
-            outbox[d] = running
+            sent = running.astype(BF16)
+            outbox[d] = sent
 
             @pl.when(d != me)
             def _():
@@ -271,13 +344,13 @@
 
             @pl.when(d == me)
             def _():
-                incoming[lax.rem(me, owners)] = running
-            return stride * running + inbox[d]
+                incoming[lax.rem(me, owners)] = sent
+            return stride * running + inbox[d].astype(F32)
 
         lax.fori_loop(0, ctx_size, pass_on, jnp.zeros((modes, own), F32))
 
+    local_first(early_pairs, chunks // 2)
     loads[6].wait()
-    span = (segment * steps).astype(F32)
 
     def out_copy(j):
         cols = pl.ds(pl.multiple_of(j * own, own), own)
@@ -290,28 +363,28 @@
             back_arrival(j).wait_recv()
         for i in range(per_owner):
             at = lanes_of(j * per_owner + i)
-            u_wide[i] = z[:, at]
             decay = decays(at)
-            weight = [jnp.broadcast_to(weight_ref[m : m + 1, at], (SEGS, LANES)) for m in range(modes)]
-            states = tuple(
-                prior[m * SEGS : (m + 1) * SEGS, at]
-                + jnp.exp(-rate_ref[m : m + 1, at] * span)
-                * incoming[j, m : m + 1, i * LANES : (i + 1) * LANES]
-                for m in range(modes)
-            )
-
-            def step(t, states):
-                rows = pl.ds(t, SEGS, stride=steps)
-                x = u_wide[i, rows, :]
-                states = tuple(decay[m] * states[m] + x for m in range(modes))
-                terms = [weight[m] * states[m] for m in range(modes)]
-                while len(terms) > 1:
-                    terms = [a + b for a, b in zip(terms[::2], terms[1::2])]
-                y_wide[i, rows, :] = terms[0]
-                return states
-
-            lax.fori_loop(0, steps, step, states, unroll=8)
-            out[:, at] = (q2[:, at].astype(F32) * y_wide[i]).astype(BF16)
+            entering = []
+            for h in range(2):
+                for m in range(modes):
+                    rate = rate_ref[m : m + 1, at]
+                    arrived = incoming[j, m : m + 1, i * LANES : (i + 1) * LANES].astype(F32)
+                    if h == 1:
+                        arrived = early_state[m : m + 1, at] + jnp.exp(-rate * taps) * arrived
+                    begin = prior[h, m * SEGS : (m + 1) * SEGS, at] + jnp.exp(-rate * span) * arrived
+                    entering.append(weights[m : m + 1, at] * begin)
+
+            def step(t, entering):
+                entering = tuple(decay[m % modes] * entering[m] for m in range(2 * modes))
+                for h in range(2):
+                    terms = entering[h * modes : (h + 1) * modes]
+                    while len(terms) > 1:
+                        terms = [a + b for a, b in zip(terms[::2], terms[1::2])]
+                    y_wide[i, pl.ds(h * taps + t, SEGS, stride=steps), :] = terms[0]
+                return entering
+
+            lax.fori_loop(0, steps, step, tuple(entering), unroll=8)
+            out[:, at] = (q2[:, at].astype(F32) * (y[:, at] + y_wide[i])).astype(BF16)
         out_copy(j).start()
 
     @pl.loop(0, owners)
@@ -332,7 +405,8 @@
 
     @pl.loop(1, tp_size)
     def _(k):
-        square_copy(k, core).wait_send()
+        square_copy(0, k, core).wait_send()
+        square_copy(1, k, core).wait_send()
 
     @pl.when(me < ctx_size - 1)
     def _():
@@ -349,7 +423,6 @@
     own = channels // owners
     chunks = channels // LANES
     table_rows = filters // chunks * taps
-    weights = li_residues * jnp.sqrt(-jnp.expm1(-2.0 * li_rates))
     wide = pltpu.VMEM((length, channels), BF16)
     dma = pltpu.SemaphoreType.DMA
     anywhere = pl.BlockSpec(memory_space=pl.ANY)
@@ -368,20 +441,25 @@
             pltpu.VMEM((filters, taps), F32),
             pltpu.VMEM((tp_size, length, LANES), F32),
             pltpu.VMEM((length, LANES), F32),
-            pltpu.VMEM((own // LANES, length, LANES), F32),
-            pltpu.VMEM((own // LANES, length, LANES), F32),
-            pltpu.VMEM((modes * SEGS, channels), F32),
-            pltpu.VMEM((owners, modes, own), F32),
-            pltpu.VMEM((ctx_size, modes, own), F32),
-            pltpu.VMEM((ctx_size, modes, own), F32),
-            pltpu.VMEM((owners, modes, own), F32),
-            dma((7,)), dma((PIECES,)), dma((PIECES,)), dma((tp_size,)), dma((tp_size,)),
+            pltpu.VMEM((max(2, own // LANES), taps, LANES), F32),
+            pltpu.VMEM((max(2, own // LANES), length, LANES), F32),
+            pltpu.VMEM((length, channels), F32),
+            pltpu.VMEM((modes, channels), F32),
+            pltpu.VMEM((2, modes * SEGS, channels), F32),
+            pltpu.VMEM((modes, channels), F32),
+            pltpu.VMEM((modes, channels), F32),
+            pltpu.VMEM((modes, LANES), F32),
+            pltpu.VMEM((owners, modes, own), BF16),
+            pltpu.VMEM((ctx_size, modes, own), BF16),
+            pltpu.VMEM((ctx_size, modes, own), BF16),
+            pltpu.VMEM((owners, modes, own), BF16),
+            dma((7,)), dma((PIECES,)), dma((PIECES,)), dma((2, tp_size)), dma((2, tp_size)),
             dma((owners,)), dma((ctx_size,)), dma((ctx_size,)), dma((owners,)), dma((owners,)),
         ],
         compiler_params=pltpu.CompilerParams(
             vmem_limit_bytes=60 << 20, collective_id=0, has_side_effects=True
         ),
-    )(q_one, k_one, v_one, q_two, k_two, mr_filter, norm_gain[None, :], li_rates, weights)
+    )(q_one, k_one, v_one, q_two, k_two, mr_filter, norm_gain[None, :], li_rates, li_residues)
 
 
 def solution(mesh):

time: 71 us -> 65.6 us (0.924)
  the two profiles are of different devices: /device:TPU:31 before, /device:TPU:0 now
where the time goes in v1:
time: 65.6 us; the launch traced here: 65.3 us
  Pallas kernels  62.2 us (95%)
  local copies, waits for them, and re-layouts  3.13 us (5%)
    pallas_call x1, Pallas kernels, on_device(): pl.pallas_call(functools.partial(whole_kernel, ctx_size, tp_size, owners)...  62.2 us
    unnamed x1, local copies, waits for them, and re-layouts  3.13 us

profile of v1, /device:TPU:0, one launch (start us, length us, event | category | flops | bytes accessed | tf_op | source)
XLA Modules:
  0.0 65.3 jit_solution(1800148808310747869)
XLA Ops:
  0.0 62.2 %shard_map.91 = bf16[256,4096]{1,0:T(8,128)(2,1)} custom-call(bf16[256,4096]{1,0:T(8,128)(2,1)} %q1_hbm.1, bf16[256,4096]{1,0:T(8,128)(2,1)} %k1_hbm.1, bf16[256,4096]{1,0:T(8,128)(2,1)} %v1_hbm.1, bf16[256,4096]{1,0:T(8,128)(2,1)} %q2_hbm.1, bf16[256,4096]{1,0:T(8,128)(2,1)} %k2_hbm.1, bf16[256,128]{1,0:T(8,128)(2,1)} %tap_ref.1, f32[1,4096]{1,0:T(1,128)} %bitcast.1, ...), custom_call_target="tpu_custom_call" | custom-call | tf_op jit(solution)/shard_map/pallas_call | solution.py:430
  62.2 3.1 %copy.11 = bf16[256,4096]{1,0:T(8,128)(2,1)} copy(bf16[256,4096]{1,0:T(8,128)(2,1)} %shard_map.91) | data formatting | bytes 4194304

commit v2 on v1

--- a/solution.py
+++ b/solution.py
@@ -43,7 +43,8 @@
     q1_hbm, k1_hbm, v1_hbm, q2_hbm, k2_hbm, tap_ref, gain_ref, rate_ref, residue_ref,
     out_hbm,
     q1, k1, v1, q2, k2, out, u_one, halo, z, early, own_table, taps_f,
-    squares, scale, u_wide, y_wide, y, weights, prior, early_state, late_state, closing,
+    squares, scale, u_wide, y_wide, y, weights, prior, early_state, late_state,
+    decay_one, decay_seg, decay_half,
     state, inbox, outbox, incoming,
     load_sem, halo_send, halo_recv, sq_send, sq_recv, in_send, in_recv, back_send, back_recv, out_sem,
 ):
@@ -124,25 +125,40 @@
     gate(first)
     loads[4].wait()
 
-    @pl.loop(0, chunks)
-    def _(c):
+    def make_tables(c, slot):
+        tap_rows = taps_f[pl.ds(pl.multiple_of(c * groups, groups), groups), :]
+        toeplitz_rows(tap_rows, groups, early.at[c], own_table.at[slot])
+
+    def main_product(c, slot):
         at = lanes_of(c)
-        tap_rows = taps_f[pl.ds(pl.multiple_of(c * groups, groups), groups), :]
-        toeplitz_rows(tap_rows, groups, early.at[c], own_table)
-        left = jnp.concatenate([early[c], own_table[...]], axis=1)
+        left = jnp.concatenate([early[c], own_table[slot]], axis=1)
         head, rest = u_one[first, at], u_one[second, at]
         right = jnp.concatenate([
             jnp.concatenate([jnp.zeros_like(head), head], axis=0),
             jnp.concatenate([head, rest], axis=0),
         ], axis=1)
-        product = jnp.dot(left, right, preferred_element_type=F32)
+        return jnp.dot(left, right, preferred_element_type=F32)
+
+    def main_store(c, product):
+        at = lanes_of(c)
         z[first, at] = pick_groups(product[:, :LANES], groups, taps)
         late = q1[second, at].astype(F32) * pick_groups(product[:, LANES:], groups, taps)
         z[second, at] = late
         squares[core, second, :] += late * late
 
+    make_tables(0, 0)
+
+    @pl.loop(0, chunks // 2)
+    def _(pair):
+        c = 2 * pair
+        product = main_product(c, 0)
+        make_tables(c + 1, 1)
+        main_store(c, product)
+        product = main_product(c + 1, 1)
+        make_tables(lax.rem(c + 2, chunks), 0)
+        main_store(c + 1, product)
+
     segment = lax.broadcasted_iota(jnp.int32, (SEGS, LANES), 0)
-    span = (segment * steps).astype(F32)
     halves = (first, second)
 
     def square_copy(h, k, slot):
@@ -169,7 +185,7 @@
         scale[halves[h], :] = jnp.broadcast_to(lax.rsqrt(total / D + 1e-06), (taps, LANES))
 
     def decays(at):
-        return [jnp.broadcast_to(jnp.exp(-rate_ref[m : m + 1, at]), (SEGS, LANES)) for m in range(modes)]
+        return [jnp.broadcast_to(decay_one[m : m + 1, at], (SEGS, LANES)) for m in range(modes)]
 
     def set_signal(h, at, i):
         scaled = z[halves[h], at] * scale[halves[h], :] * gain_ref[:, at]
@@ -207,7 +223,7 @@
         return lax.fori_loop(0, steps, step, zero_states, unroll=16)
 
     def join_segments(h, at, m, inclusive):
-        factor = jnp.exp(-rate_ref[m : m + 1, at] * steps)
+        factor = jnp.broadcast_to(decay_seg[m : m + 1, at], (SEGS, LANES))
         shift = 1
         while shift < SEGS:
             moved = jnp.where(segment >= shift, pltpu.roll(inclusive, shift, 0), 0.0)
@@ -217,7 +233,7 @@
         prior[h, m * SEGS : (m + 1) * SEGS, at] = jnp.where(
             segment >= 1, pltpu.roll(inclusive, 1, 0), 0.0
         )
-        return inclusive[SEGS - 1 :, :], factor
+        return inclusive[SEGS - 1 :, :]
 
     send_squares(1)
 
@@ -230,6 +246,13 @@
             series = 1.0 - double * series * (1.0 / order)
         gap = jnp.where(double < 0.5, double * series, 1.0 - jnp.exp(-double))
         weights[:, at] = residue_ref[:, at] * jnp.sqrt(gap)
+        decay_one[:, at] = jnp.exp(-rate_ref[:, at])
+        per_segment = jnp.exp(-rate_ref[:, at] * steps)
+        decay_seg[:, at] = per_segment
+        per_half = per_segment
+        for _ in range(3):
+            per_half = per_half * per_half
+        decay_half[:, at] = per_half
 
     loads[5].wait()
     find_scale(1)
@@ -241,7 +264,7 @@
             set_signal(1, at, i)
             states = local_pass(1, at, i)
             for m in range(modes):
-                last, _ = join_segments(1, at, m, states[m])
+                last = join_segments(1, at, m, states[m])
                 late_state[m : m + 1, at] = last
 
     pairs = chunks // PIECES // 2
@@ -284,10 +307,10 @@
             set_signal(0, at, i)
             states = closing_pass(at, i)
             for m in range(modes):
-                last, factor = join_segments(0, at, m, states[m])
+                last = join_segments(0, at, m, states[m])
                 early_state[m : m + 1, at] = last
-                closing[m : m + 1, :] = factor * last + late_state[m : m + 1, at]
-            state[j, :, i * LANES : (i + 1) * LANES] = closing[...].astype(BF16)
+            closing = decay_half[:, at] * early_state[:, at] + late_state[:, at]
+            state[j, :, i * LANES : (i + 1) * LANES] = closing.astype(BF16)
 
         @pl.when(j != me)
         def _():
@@ -364,15 +387,20 @@
         for i in range(per_owner):
             at = lanes_of(j * per_owner + i)
             decay = decays(at)
-            entering = []
-            for h in range(2):
-                for m in range(modes):
-                    rate = rate_ref[m : m + 1, at]
-                    arrived = incoming[j, m : m + 1, i * LANES : (i + 1) * LANES].astype(F32)
-                    if h == 1:
-                        arrived = early_state[m : m + 1, at] + jnp.exp(-rate * taps) * arrived
-                    begin = prior[h, m * SEGS : (m + 1) * SEGS, at] + jnp.exp(-rate * span) * arrived
-                    entering.append(weights[m : m + 1, at] * begin)
+            arrived = incoming[j, :, i * LANES : (i + 1) * LANES].astype(F32)
+            later = early_state[:, at] + decay_half[:, at] * arrived
+            weight = weights[:, at]
+            heads = ([], [])
+            for m in range(modes):
+                one = jnp.broadcast_to(decay_seg[m : m + 1, at], (SEGS, LANES))
+                two = one * one
+                lift = jnp.where(segment % 2 == 1, one, 1.0)
+                lift = lift * jnp.where(segment // 2 % 2 == 1, two, 1.0)
+                lift = lift * jnp.where(segment // 4 % 2 == 1, two * two, 1.0)
+                for h, carried in enumerate((arrived, later)):
+                    begin = prior[h, m * SEGS : (m + 1) * SEGS, at] + lift * carried[m : m + 1, :]
+                    heads[h].append(weight[m : m + 1, :] * begin)
+            entering = heads[0] + heads[1]
 
             def step(t, entering):
                 entering = tuple(decay[m % modes] * entering[m] for m in range(2 * modes))
@@ -437,7 +465,7 @@
             pltpu.VMEM((taps, channels), BF16),
             pltpu.VMEM((length, channels), F32),
             pltpu.VMEM((chunks, table_rows, taps), BF16),
-            pltpu.VMEM((table_rows, taps), BF16),
+            pltpu.VMEM((2, table_rows, taps), BF16),
             pltpu.VMEM((filters, taps), F32),
             pltpu.VMEM((tp_size, length, LANES), F32),
             pltpu.VMEM((length, LANES), F32),
@@ -448,7 +476,9 @@
             pltpu.VMEM((2, modes * SEGS, channels), F32),
             pltpu.VMEM((modes, channels), F32),
             pltpu.VMEM((modes, channels), F32),
-            pltpu.VMEM((modes, LANES), F32),
+            pltpu.VMEM((modes, channels), F32),
+            pltpu.VMEM((modes, channels), F32),
+            pltpu.VMEM((modes, channels), F32),
             pltpu.VMEM((owners, modes, own), BF16),
             pltpu.VMEM((ctx_size, modes, own), BF16),
             pltpu.VMEM((ctx_size, modes, own), BF16),

time: 65.6 us -> 61 us (0.930)
  Pallas kernels: 62.2 us -> 57.6 us
    pallas_call x1, Pallas kernels: 62.2 us -> 57.6 us  [on_device(): pl.pallas_call(functools.partial(whole_kernel, ctx_size, tp_size, owners)...]
where the time goes in v2:
time: 61 us; the launch traced here: 60.7 us
  Pallas kernels  57.6 us (94%)
  local copies, waits for them, and re-layouts  3.13 us (5%)
    pallas_call x1, Pallas kernels, on_device(): pl.pallas_call(functools.partial(whole_kernel, ctx_size, tp_size, owners)...  57.6 us
    unnamed x1, local copies, waits for them, and re-layouts  3.13 us

profile of v2, /device:TPU:0, one launch (start us, length us, event | category | flops | bytes accessed | tf_op | source)
XLA Modules:
  0.0 60.7 jit_solution(480431251139081214)
XLA Ops:
  0.0 57.6 %shard_map.91 = bf16[256,4096]{1,0:T(8,128)(2,1)} custom-call(bf16[256,4096]{1,0:T(8,128)(2,1)} %q1_hbm.1, bf16[256,4096]{1,0:T(8,128)(2,1)} %k1_hbm.1, bf16[256,4096]{1,0:T(8,128)(2,1)} %v1_hbm.1, bf16[256,4096]{1,0:T(8,128)(2,1)} %q2_hbm.1, bf16[256,4096]{1,0:T(8,128)(2,1)} %k2_hbm.1, bf16[256,128]{1,0:T(8,128)(2,1)} %tap_ref.1, f32[1,4096]{1,0:T(1,128)} %bitcast.1, ...), custom_call_target="tpu_custom_call" | custom-call | tf_op jit(solution)/shard_map/pallas_call | solution.py:458
  57.6 3.1 %copy.11 = bf16[256,4096]{1,0:T(8,128)(2,1)} copy(bf16[256,4096]{1,0:T(8,128)(2,1)} %shard_map.91) | data formatting | bytes 4194304
